TPU v7x, 512 devices: a whole 4x4x16 slice. The times are simulated.
512 devices in a mesh: chan: 32 (over z, y_lo), row: 2 (over core), col: 8 (over x, y_hi).
Axes of the slice: x: 4, y: 4 (y_hi: 2, y_lo: 2; y = y_hi * 2 + y_lo), z: 16, core: 2. Of those that a mesh axis runs over, the one named last changes fastest.
Arguments:
- volts: bfloat16 [2, 1024, 2, 52736], P(None, ('chan', 'row', 'col')), may hold values from -6 to 6
- taps: float32 [8, 512], replicated, may hold values from -2 to 2
- owner_map: int32 [384], replicated, may hold values from 0 to 255, as said below
- assign: int32 [512], replicated, may hold values from 0 to 511, each once
Outputs:
- visibility: bfloat16 [512, 2, 1024, 1024], P(('chan', 'col'), None, 'row')
Inputs may be any that keep to these rules, and one draw needn't show every extreme that they name: `owner_map`: each owner holds 1 to 2 channels, and some owner holds exactly 2. `assign`: A permutation of the stations.
All inputs are finite; a program needn't handle non-finite values.
Results may differ from a plain program's by a relative error of at most 0.0055.
Values may be sent and summed in bfloat16 or wider, within the bound.
A program may use at most 64 MiB of HBM per device.

v0:
```python
import math

import jax
import jax.numpy as jnp
from jax import lax
from jax.sharding import PartitionSpec as P

STATIONS = 512
NFFT = 512
TAPS = 8
BATCHES = 2
CAP = 2


def slot_table(owner_map, owner_count, slot_count):
    channel_count = owner_map.shape[0]
    ranking = jnp.argsort(owner_map * channel_count + jnp.arange(channel_count, dtype=jnp.int32))
    counts = jnp.sum(
        (owner_map[None, :] == jnp.arange(owner_count, dtype=jnp.int32)[:, None]).astype(jnp.int32),
        axis=1,
    )
    starts = jnp.cumsum(counts) - counts
    slot_index = jnp.arange(slot_count, dtype=jnp.int32)
    position = jnp.clip(starts[:, None] + slot_index[None, :], 0, channel_count - 1)
    channel = jnp.take(ranking, position, axis=0)
    is_live = slot_index[None, :] < counts[:, None]
    return (channel, is_live)


def shards(volts, taps, owner_map, assign):
    chan_count = lax.axis_size("chan")
    rows_count = lax.axis_size("row")
    cols_count = lax.axis_size("col")
    owner_count = chan_count * cols_count
    local_inputs = volts.shape[1]
    spec_len = volts.shape[3] // NFFT - TAPS + 1
    channel, is_live = slot_table(owner_map, owner_count, CAP)
    points = jnp.arange(NFFT, dtype=jnp.int32)
    phase = (points[:, None, None] * channel.T[None, :, :] % NFFT).astype(jnp.float32) * (
        2.0 * math.pi / NFFT
    )
    weight_live = is_live.T[None, :, :].astype(jnp.float32) / math.sqrt(NFFT)
    cosine = jnp.cos(phase) * weight_live
    sine = jnp.sin(phase) * weight_live
    table = jnp.stack(
        [jnp.stack([cosine, -sine], axis=1), jnp.stack([sine, cosine], axis=1)], axis=0
    )
    total_inputs = 2 * STATIONS
    positions = jnp.arange(total_inputs, dtype=jnp.int32)
    pick = 2 * jnp.take(assign, positions // 2, axis=0) + positions % 2
    device_of = pick // local_inputs
    within = pick % local_inputs
    chan_of = device_of // (rows_count * cols_count)
    row_of = device_of // cols_count % rows_count
    col_of = device_of % cols_count
    located = ((row_of * cols_count + col_of) * chan_count + chan_of) * local_inputs + within
    row_count = total_inputs // rows_count
    row_pick = lax.dynamic_slice_in_dim(located, lax.axis_index("row") * row_count, row_count)
    total = jnp.zeros((CAP, 2 * row_count, total_inputs), jnp.float32)
    for batch in range(BATCHES):
        signal = (
            volts[batch].astype(jnp.float32).reshape(local_inputs, 2, spec_len + TAPS - 1, NFFT)
        )
        summed = jnp.zeros((local_inputs, 2, spec_len, NFFT), jnp.float32)
        for tap_index in range(TAPS):
            summed = (
                summed
                + taps[tap_index][None, None, None, :]
                * signal[:, :, tap_index : tap_index + spec_len, :]
            )
        result = jnp.einsum("iasj,ajbkg->kgibs", summed, table, precision=lax.Precision.HIGHEST)
        turned = lax.all_to_all(
            lax.all_to_all(
                result.reshape(CAP, chan_count, cols_count, local_inputs, 2 * spec_len).astype(
                    jnp.bfloat16
                ),
                "chan",
                split_axis=1,
                concat_axis=3,
                tiled=True,
            ),
            "col",
            split_axis=2,
            concat_axis=3,
            tiled=True,
        )
        gathered = lax.all_gather(turned, "row", axis=3, tiled=True)
        flat = gathered.reshape(CAP, total_inputs, -1)
        width = flat.shape[2]
        rows = jnp.take(flat, row_pick, axis=1)
        split_rows = rows.reshape(CAP, row_count, width // (2 * spec_len), 2, spec_len)
        flipped = jnp.stack(
            [split_rows[:, :, :, 1, :], -split_rows[:, :, :, 0, :]], axis=3
        ).reshape(CAP, row_count, width)
        stacked = jnp.concatenate([rows, flipped], axis=1)
        columns = jnp.take(flat, located, axis=1)
        total = total + jnp.einsum(
            "kpx,kqx->kpq", stacked, columns, preferred_element_type=jnp.float32
        )
    scale = 1.0 / math.sqrt(2 * BATCHES * spec_len)
    return (total * scale).reshape(CAP, 2, row_count, total_inputs).astype(jnp.bfloat16)


def solution(mesh):
    placed = (P(None, ("chan", "row", "col"), None, None), P(), P(), P())
    return jax.shard_map(
        shards,
        mesh=mesh,
        in_specs=placed,
        out_specs=P(("chan", "col"), None, "row", None),
        check_vma=False,
    )
```

profile of v0, /device:TPU:1, one launch (start us, length us, event | category | flops | bytes accessed | tf_op | source)
XLA Modules:
  0.0 180.4 jit_solution(5233471085927798527)
XLA Ops:
  0.0 0.8 convert_reduce_fusion
  0.8 0.7 iota_add_fusion
  1.5 0.3 reduce-window.9
  2.1 1.0 fusion.107
  3.3 0.1 reshape.329
  3.4 3.8 %sort.17 = (s32[384]{0:T(512)}, s32[384]{0:T(512)S(1)}) sort(s32[384]{0:T(512)S(1)} %iota_add_fusion, s32[384]{0:T(512)S(1)} %iota.40), dimensions={0}, to_apply=%region_3.4 | sort | flops 3456 | bytes 6144 | tf_op jit(solution)/shard_map/jit(argsort)/sort | solution.py:17
  7.2 3.5 %gather_fusion = s32[512]{0:T(512)S(1)} fusion(s32[384]{0:T(512)S(1)} %get-tuple-element.8, s32[1024]{0:T(1024)S(1)} %pad_clamp_fusion.1), kind=kCustom, calls=%fused_computation.4 | custom fusion | bytes 6144 | tf_op jit(solution)/shard_map/jit(_take)/gather | solution.py:25
  10.7 0.1 reshape.328
  11.1 0.6 slice_convert_fusion
  11.7 1.5 reshape.293
  13.2 4.2 %fusion.71 = (f32[512,1,2,256]{3,0,2,1:T(8,128)S(1)}, f32[512,1,2,256]{3,0,2,1:T(8,128)S(1)}, f32[512,1,2,256]{3,0,2,1:T(8,128)S(1)}) fusion(f32[2,256]{1,0:T(2,128)S(1)} %compare_select_fusion.6, s32[2,256]{1,0:T(2,128)S(1)} %copy.54), kind=kLoop, calls=%fused_computation.100 | loop fusion | flops 4456448 | bytes 3149824 | tf_op jit(solution)/shard_map/neg | solution.py:46
  17.4 0.3 maximum_bitcast_fusion.3
  17.7 1.3 copy-done.1
  19.0 4.6 %fusion.6 = bf16[2,256,2,2,96]{1,4,2,0,3:T(8,128)(2,1)} fusion(f32[1,512,2,2,256]{4,1,0,3,2:T(8,128)S(1)} %get-tuple-element.14, f32[1,512,2,2,256]{4,1,0,3,2:T(8,128)S(1)} %get-tuple-element.13, f32[2,2,103,512]{3,2,1,0:T(8,128)S(1)} %copy-done.2, f32[512]{0:T(512)S(1)} %bitcast.127, f32[512]{0:T(512)S(1)} %bitcast.129, f32[512]{0:T(512)S(1)} %bitcast.117, ...), kind=kOutput, calls=%fused_computation.21 | convolution fusion | flops 2420113408 | bytes 10895360 | tf_op jit(solution)/shard_map/iasj,ajbkg->kgibs/dot_general | solution.py:71
  23.7 1.3 copy.56
  25.0 1.1 convert_element_type.68
  26.1 1.9 %copy.57 = bf16[2,32,8,2,192]{4,2,3,0,1:T(8,128)(2,1)} copy(bf16[2,32,8,2,192]{4,2,1,3,0:T(8,128)(2,1)} %convert_element_type.68) | data formatting | bytes 786432 | tf_op jit(solution)/shard_map/convert_element_type | solution.py:74
  28.0 17.0 %all-to-all-start = ((bf16[2,32,8,2,192]{4,2,3,0,1:T(8,128)(2,1)}), bf16[2,32,8,2,192]{4,2,3,0,1:T(8,128)(2,1)S(1)}, u32[]{:S(2)}, u32[]{:S(2)}) async-start(bf16[2,32,8,2,192]{4,2,3,0,1:T(8,128)(2,1)} %copy.57), calls=%async_computation | async-start | bytes 1048576 | tf_op jit(solution)/shard_map/all_to_all | solution.py:73
  45.1 1.5 reshape.294
  46.6 9.2 %fusion.7 = bf16[2,256,2,2,96]{1,4,2,0,3:T(8,128)(2,1)} fusion(f32[1,512,2,2,256]{4,1,0,3,2:T(8,128)} %copy-done.1, f32[1,512,2,2,256]{4,1,0,3,2:T(8,128)S(1)} %get-tuple-element.13, f32[2,2,103,512]{3,2,1,0:T(8,128)} %reshape.294, f32[512]{0:T(512)S(1)} %bitcast.128, f32[512]{0:T(512)S(1)} %bitcast.130, f32[512]{0:T(512)S(1)} %bitcast.118, ...), kind=kOutput, calls=%fused_computation.22 | convolution fusion | flops 2420113408 | bytes 10895360 | tf_op jit(solution)/shard_map/iasj,ajbkg->kgibs/dot_general | solution.py:71
  55.8 1.3 copy.65
  57.1 0.3 convert_element_type.73
  57.4 0.9 copy.66
  58.3 17.8 %all-to-all-done = bf16[2,32,8,2,192]{4,2,3,0,1:T(8,128)(2,1)S(1)} async-done(((bf16[2,32,8,2,192]{4,2,3,0,1:T(8,128)(2,1)}), bf16[2,32,8,2,192]{4,2,3,0,1:T(8,128)(2,1)S(1)}, u32[]{:S(2)}, u32[]{:S(2)}) %all-to-all-start) | async-done | bytes 393248 | tf_op jit(solution)/shard_map/all_to_all | solution.py:73
  76.0 5.2 %all-to-all-start.2 = ((bf16[2,32,8,2,192]{4,2,3,0,1:T(8,128)(2,1)}), bf16[2,32,8,2,192]{4,2,3,0,1:T(8,128)(2,1)S(1)}, u32[]{:S(2)}, u32[]{:S(2)}) async-start(bf16[2,32,8,2,192]{4,2,3,0,1:T(8,128)(2,1)} %copy.66), calls=%async_computation.2 | async-start | bytes 1048576 | tf_op jit(solution)/shard_map/all_to_all | solution.py:73
  81.3 0.9 copy.59
  82.3 29.5 %all-to-all-done.2 = bf16[2,32,8,2,192]{4,2,3,0,1:T(8,128)(2,1)S(1)} async-done(((bf16[2,32,8,2,192]{4,2,3,0,1:T(8,128)(2,1)}), bf16[2,32,8,2,192]{4,2,3,0,1:T(8,128)(2,1)S(1)}, u32[]{:S(2)}, u32[]{:S(2)}) %all-to-all-start.2) | async-done | bytes 393248 | tf_op jit(solution)/shard_map/all_to_all | solution.py:73
  111.7 6.3 %all-to-all-start.1 = ((bf16[2,1,8,64,192]{4,3,0,1,2:T(8,128)(2,1)}), bf16[2,1,8,64,192]{4,3,0,1,2:T(8,128)(2,1)S(1)}, u32[]{:S(2)}, u32[]{:S(2)}) async-start(bf16[2,1,8,64,192]{4,3,0,1,2:T(8,128)(2,1)} %copy.59), calls=%async_computation.1 | async-start | bytes 1048576 | tf_op jit(solution)/shard_map/all_to_all | solution.py:72
  118.1 6.9 %gather_fusion.1 = s32[1024]{0:T(1024)S(1)} fusion(s32[512]{0:T(512)S(1)} %copy-done, s32[1024]{0:T(1024)S(1)} %broadcast_clamp_fusion), kind=kCustom, calls=%fused_computation.5 | custom fusion | bytes 12288 | tf_op jit(solution)/shard_map/jit(_take)/gather | solution.py:50
  125.0 0.9 copy.68
  125.9 0.7 all-to-all-done.1
  126.6 6.0 %all-to-all-start.3 = ((bf16[2,1,8,64,192]{4,3,0,1,2:T(8,128)(2,1)}), bf16[2,1,8,64,192]{4,3,0,1,2:T(8,128)(2,1)S(1)}, u32[]{:S(2)}, u32[]{:S(2)}) async-start(bf16[2,1,8,64,192]{4,3,0,1,2:T(8,128)(2,1)} %copy.68), calls=%async_computation.3 | async-start | bytes 1048576 | tf_op jit(solution)/shard_map/all_to_all | solution.py:72
  132.7 0.2 copy.61
  132.9 8.2 %all-to-all-done.3 = bf16[2,1,8,64,192]{4,3,0,1,2:T(8,128)(2,1)S(1)} async-done(((bf16[2,1,8,64,192]{4,3,0,1,2:T(8,128)(2,1)}), bf16[2,1,8,64,192]{4,3,0,1,2:T(8,128)(2,1)S(1)}, u32[]{:S(2)}, u32[]{:S(2)}) %all-to-all-start.3) | async-done | bytes 393248 | tf_op jit(solution)/shard_map/all_to_all | solution.py:72
  141.2 0.2 copy.70
  141.4 7.5 %all_gather.7 = bf16[2,1,1,1024,192]{3,4,2,1,0:T(8,128)(2,1)S(1)} all-gather(bf16[2,1,1,512,192]{3,4,2,1,0:T(8,128)(2,1)S(1)} %copy.70), channel_id=1, replica_groups=mesh['chan'=32,'row'=2,'col'=8] {'row'}, dimensions={3}, use_global_device_ids=true | all-gather | bytes 1179648 | tf_op jit(solution)/shard_map/all_gather | solution.py:87
  148.9 0.9 copy.71
  149.8 2.6 %all_gather.6 = bf16[2,1,1,1024,192]{3,4,2,1,0:T(8,128)(2,1)S(1)} all-gather(bf16[2,1,1,512,192]{3,4,2,1,0:T(8,128)(2,1)S(1)} %copy.61), channel_id=1, replica_groups=mesh['chan'=32,'row'=2,'col'=8] {'row'}, dimensions={3}, use_global_device_ids=true | all-gather | bytes 1179648 | tf_op jit(solution)/shard_map/all_gather | solution.py:87
  152.4 0.9 copy.62
  153.3 3.0 %gather_fusion.2 = bf16[512,2,192]{2,1,0:T(2,128)(2,1)} fusion(bf16[2,1024,192]{2,0,1:T(2,128)(2,1)S(1)} %bitcast.101, s32[1024]{0:T(1024)S(1)} %pad_clamp_fusion), kind=kCustom, calls=%fused_computation.clone | custom fusion | bytes 788480 | tf_op jit(solution)/shard_map/jit(_take)/gather | solution.py:90
  156.3 4.2 %gather_fusion.3 = bf16[1024,2,192]{2,1,0:T(2,128)(2,1)S(1)} fusion(bf16[2,1024,192]{2,0,1:T(2,128)(2,1)S(1)} %bitcast.102, s32[1024]{0:T(1024)S(1)} %fusion.99), kind=kCustom, calls=%fused_computation.1.clone | custom fusion | bytes 1576960 | tf_op jit(solution)/shard_map/jit(_take)/gather | solution.py:96
  160.5 3.0 %gather_fusion.4 = bf16[512,2,192]{2,1,0:T(2,128)(2,1)} fusion(bf16[2,1024,192]{2,0,1:T(2,128)(2,1)S(1)} %bitcast.99, s32[1024]{0:T(1024)S(1)} %pad_clamp_fusion), kind=kCustom, calls=%fused_computation.2.clone | custom fusion | bytes 788480 | tf_op jit(solution)/shard_map/jit(_take)/gather | solution.py:90
  163.5 4.2 %gather_fusion.5 = bf16[1024,2,192]{2,1,0:T(2,128)(2,1)S(1)} fusion(bf16[2,1024,192]{2,0,1:T(2,128)(2,1)S(1)} %bitcast.100, s32[1024]{0:T(1024)S(1)} %fusion.99), kind=kCustom, calls=%fused_computation.3.clone | custom fusion | bytes 1576960 | tf_op jit(solution)/shard_map/jit(_take)/gather | solution.py:96
  167.7 1.3 copy.63
  169.0 1.3 copy.72
  170.5 4.2 %fusion.17 = (bf16[2,1024,192]{2,0,1:T(2,128)(2,1)S(1)}, bf16[2,1024,192]{2,0,1:T(2,128)(2,1)S(1)}) fusion(bf16[1024,2,192]{2,1,0:T(2,128)(2,1)S(1)} %gather_fusion.5, pred[1024]{0:T(1024)(128)(4,1)S(1)} %get-tuple-element.11, bf16[1024,2,192]{2,1,0:T(2,128)(2,1)S(1)} %gather_fusion.3), kind=kLoop, calls=%fused_computation.34 | loop fusion | flops 786432 | bytes 3146752 | tf_op jit(solution)/shard_map/jit(_take)/select_n | solution.py:96
  174.8 1.6 fusion.12
  176.3 4.0 %multiply_convert_fusion = bf16[2,1024,1024]{2,1,0:T(8,128)(2,1)} fusion(f32[2,1024,1024]{2,1,0:T(8,128)S(1)} %fusion.12, bf16[2,1024,192]{2,0,1:T(2,128)(2,1)S(1)} %get-tuple-element.32, bf16[2,512,192]{1,2,0:T(8,128)(2,1)S(1)} %bitcast.111, bf16[2,512,192]{1,2,0:T(8,128)(2,1)S(1)} %bitcast.104), kind=kOutput, calls=%fused_computation.6 | convolution fusion | flops 813170688 | bytes 14155776 | tf_op jit(solution)/shard_map/kpx,kqx->kpq/dot_general | solution.py:97
  (32 shorter events, 1.1 us)
Async XLA Ops:
  0.0 118.1 %copy-start = (s32[512]{0:T(512)S(1)}, s32[512]{0:T(512)}, u32[]{:S(2)}) copy-start(s32[512]{0:T(512)} %param.11) | copy-start | bytes 6148
  7.2 3.9 %copy-start.3 = (bf16[2,2,2,52736]{3,2,1,0:T(2,128)(2,1)S(1)}, bf16[2,2,2,52736]{3,2,1,0:T(2,128)(2,1)}, u32[]{:S(2)}) copy-start(bf16[2,2,2,52736]{3,2,1,0:T(2,128)(2,1)} %param.8) | copy-start | bytes 2531332
  17.4 1.6 copy-start.2
  17.7 1.3 copy-start.1
  28.0 48.0 %all-to-all-start = ((bf16[2,32,8,2,192]{4,2,3,0,1:T(8,128)(2,1)}), bf16[2,32,8,2,192]{4,2,3,0,1:T(8,128)(2,1)S(1)}, u32[]{:S(2)}, u32[]{:S(2)}) async-start(bf16[2,32,8,2,192]{4,2,3,0,1:T(8,128)(2,1)} %copy.57), calls=%async_computation | async-start | bytes 1048576 | tf_op jit(solution)/shard_map/all_to_all | solution.py:73
  76.0 35.7 %all-to-all-start.2 = ((bf16[2,32,8,2,192]{4,2,3,0,1:T(8,128)(2,1)}), bf16[2,32,8,2,192]{4,2,3,0,1:T(8,128)(2,1)S(1)}, u32[]{:S(2)}, u32[]{:S(2)}) async-start(bf16[2,32,8,2,192]{4,2,3,0,1:T(8,128)(2,1)} %copy.66), calls=%async_computation.2 | async-start | bytes 1048576 | tf_op jit(solution)/shard_map/all_to_all | solution.py:73
  111.7 14.9 %all-to-all-start.1 = ((bf16[2,1,8,64,192]{4,3,0,1,2:T(8,128)(2,1)}), bf16[2,1,8,64,192]{4,3,0,1,2:T(8,128)(2,1)S(1)}, u32[]{:S(2)}, u32[]{:S(2)}) async-start(bf16[2,1,8,64,192]{4,3,0,1,2:T(8,128)(2,1)} %copy.59), calls=%async_computation.1 | async-start | bytes 1048576 | tf_op jit(solution)/shard_map/all_to_all | solution.py:72
  126.6 14.5 %all-to-all-start.3 = ((bf16[2,1,8,64,192]{4,3,0,1,2:T(8,128)(2,1)}), bf16[2,1,8,64,192]{4,3,0,1,2:T(8,128)(2,1)S(1)}, u32[]{:S(2)}, u32[]{:S(2)}) async-start(bf16[2,1,8,64,192]{4,3,0,1,2:T(8,128)(2,1)} %copy.68), calls=%async_computation.3 | async-start | bytes 1048576 | tf_op jit(solution)/shard_map/all_to_all | solution.py:72
where the time goes:
time: 181 us; the launch traced here: 180 us
  waiting for transfers between devices  56.1 us (31%)
  local copies, waits for them, and re-layouts  44.2 us (24%)
  starting transfers between devices  34.6 us (19%)
  matrix products  19.4 us (11%)
  other arithmetic  15.6 us (9%)
  blocking collectives  10.1 us (6%)
    all_to_all x2, waiting for transfers between devices, shards(): lax.all_to_all(result.reshape(CAP, chan_count, cols_count, local_inputs,...  47.3 us
    all_to_all x2, starting transfers between devices, shards(): lax.all_to_all(result.reshape(CAP, chan_count, cols_count, local_inputs,...  22.3 us
    dot_general x2, matrix products, shards(): jnp.einsum('iasj,ajbkg->kgibs', summed, table, precision=lax.Precision.HI...  13.8 us
    all_to_all x2, starting transfers between devices, shards(): lax.all_to_all(lax.all_to_all(result.reshape(CAP, chan_count, cols_count,...  12.3 us
    all_gather x2, blocking collectives, shards(): gathered = lax.all_gather(turned, 'row', axis=3, tiled=True)  10.1 us
    all_to_all x2, waiting for transfers between devices, shards(): lax.all_to_all(lax.all_to_all(result.reshape(CAP, chan_count, cols_count,...  8.86 us
    gather x4, local copies, waits for them, and re-layouts, shards(): rows = jnp.take(flat, row_pick, axis=1)  8.64 us
    gather x2, local copies, waits for them, and re-layouts, shards(): columns = jnp.take(flat, located, axis=1)  8.33 us
  transfers between devices with their start and end apart: 4, of which 4 were waited for; matrix products, arithmetic and copies ran while one was open for 12% of the time, Pallas kernels for 0%

commit v1 on v0

v1 whole, which is shorter than its diff:
```python
import functools
import math

import jax
import jax.numpy as jnp
import ml_dtypes
import numpy as np
from jax import lax
from jax.experimental import pallas as pl
from jax.experimental.pallas import tpu as pltpu
from jax.sharding import PartitionSpec as P

NFFT = 512
TAPS = 8
BATCHES = 2
SPEC_B = 96
NCHAN = 384
BLOCKS = SPEC_B + TAPS - 1
SPEC = BATCHES * SPEC_B
WIDTH = 2 * SPEC
MESH = pl.DeviceIdType.MESH


def dft_tables():
    phase = 2.0 * np.pi / NFFT * (np.outer(np.arange(NCHAN), np.arange(NFFT)) % NFFT)
    both = np.stack([np.cos(phase), np.sin(phase)], axis=1) / math.sqrt(NFFT)
    both = both.reshape(NCHAN, 2, 4, 128).transpose(0, 2, 1, 3).reshape(NCHAN, 2 * NFFT)
    high = both.astype(np.float32).astype(ml_dtypes.bfloat16)
    low = (both - high.astype(np.float64)).astype(np.float32).astype(ml_dtypes.bfloat16)
    return high, low


def rows_by(left, right):
    return lax.dot_general(
        left, right, (((1,), (1,)), ((), ())), preferred_element_type=jnp.float32
    )


def times(left, right):
    return jnp.dot(left, right, preferred_element_type=jnp.float32)


def one_hot(found):
    return jnp.where(found, 1.0, 0.0).astype(jnp.bfloat16)


def exchange_kernel(
    volts, taps, owner, assign, table_hi, table_lo, out,
    vbuf, tap_v, tapx, own_v, asg_v, thi, tlo, filt, ghi, glo, wsel, perm, hot_a, hot_b,
    send_a, send_b, recv_a, recv_b, stage_a, stage_b, x_a, x_b, spread,
    lsem, za_s, za_r, xb_s, xb_r, zb_s, zb_r, xa_s, xa_r, fa_s, fa_r, fb_s, fb_r,
):
    chan, row, col = lax.axis_index("chan"), lax.axis_index("row"), lax.axis_index("col")
    z, o = chan // 2, chan % 2 * 8 + col

    def device(zz, oo, rr):
        return (zz * 2 + oo // 8, rr, oo % 8)

    def later(base, step):
        return lax.rem(base + step, 16)

    barrier = pltpu.get_barrier_semaphore()

    def greet(d, carry):
        pl.semaphore_signal(barrier, inc=1, device_id=device(later(z, d), o, row), device_id_type=MESH)
        pl.semaphore_signal(barrier, inc=1, device_id=device(z, later(o, d), row), device_id_type=MESH)
        return carry

    lax.fori_loop(1, 16, greet, 0)
    pl.semaphore_signal(barrier, inc=1, device_id=device(z, o, 1 - row), device_id_type=MESH)

    loads = [
        pltpu.make_async_copy(volts.at[:, 0], vbuf.at[0], lsem.at[0]),
        pltpu.make_async_copy(volts.at[:, 1], vbuf.at[1], lsem.at[1]),
        pltpu.make_async_copy(taps, tap_v, lsem.at[2]),
        pltpu.make_async_copy(owner, own_v, lsem.at[3]),
        pltpu.make_async_copy(assign, asg_v, lsem.at[4]),
        pltpu.make_async_copy(table_hi, thi, lsem.at[5]),
        pltpu.make_async_copy(table_lo, tlo, lsem.at[6]),
    ]
    for k in (3, 2, 0, 5, 6, 1, 4):
        loads[k].start()

    def far(i):
        return 8 + (1 - 2 * lax.rem(i, 2)) * ((i + 1) // 2)

    def copy_za(d):
        t = later(z, d)
        return pltpu.make_async_remote_copy(
            send_a.at[t], recv_a.at[z], za_s.at[d], za_r.at[d], device_id=device(t, o, row), device_id_type=MESH)

    def copy_xb(d):
        t = later(o, d)
        return pltpu.make_async_remote_copy(
            send_b.at[t], recv_b.at[o], xb_s.at[d], xb_r.at[d], device_id=device(z, t, row), device_id_type=MESH)

    def copy_zb(d):
        t = later(z, d)
        return pltpu.make_async_remote_copy(
            stage_b.at[t], x_b.at[row * 16 + z], zb_s.at[d], zb_r.at[d], device_id=device(t, o, row), device_id_type=MESH)

    def copy_xa(d):
        t = later(o, d)
        return pltpu.make_async_remote_copy(
            stage_a.at[t], x_a.at[row * 16 + o], xa_s.at[d], xa_r.at[d], device_id=device(z, t, row), device_id_type=MESH)

    def forward_a():
        half = pl.ds(row * 16, 16)
        return pltpu.make_async_remote_copy(
            x_a.at[half], x_a.at[half], fa_s, fa_r, device_id=device(z, o, 1 - row), device_id_type=MESH)

    def forward_b(block):
        return pltpu.make_async_remote_copy(
            x_b.at[row * 16 + block], x_b.at[row * 16 + block], fb_s.at[block], fb_r.at[block],
            device_id=device(z, o, 1 - row), device_id_type=MESH)

    def each(action):
        def step(i, carry):
            action(far(i))
            return carry

        lax.fori_loop(0, 15, step, 0)

    def choose(swapped):
        line = lax.broadcasted_iota(jnp.int32, (256, NCHAN), 0)
        owner_of_line = (line % 16) * 16 + line // 16 if swapped else line
        owned = jnp.where(own_v[...].reshape(1, NCHAN) == owner_of_line, 1.0, 0.0)
        before = jnp.where(
            lax.broadcasted_iota(jnp.int32, (NCHAN, NCHAN), 0)
            < lax.broadcasted_iota(jnp.int32, (NCHAN, NCHAN), 1), 1.0, 0.0).astype(jnp.bfloat16)
        earlier = times(owned.astype(jnp.bfloat16), before)
        for slot in range(2):
            taken = jnp.where(earlier == float(slot), owned, 0.0).astype(jnp.bfloat16)
            wsel[:, slot * 16 : slot * 16 + 16, :] = taken.reshape(16, 16, NCHAN)

    def spectra(pol):
        loads[pol].wait()
        if pol == 0:
            loads[2].wait()
            for m in range(TAPS):
                for j in range(4):
                    line = tap_v[m : m + 1, j * 128 : j * 128 + 128]
                    tapx[m, 2 * j : 2 * j + 2, :] = jnp.broadcast_to(line, (2, 128))
        weights = [tapx[m] for m in range(TAPS)]

        def chunk(i, carry):
            first = i * 8
            for b in range(BATCHES):
                signal = [vbuf[pol, b, first + t].astype(jnp.float32) for t in range(15)]
                for s in range(8):
                    total = weights[0] * signal[s]
                    for m in range(1, TAPS):
                        total = total + weights[m] * signal[s + m]
                    filt[pl.ds(pl.multiple_of((b * SPEC_B + first + s) * 8, 8), 8), :] = total
            return carry

        lax.fori_loop(0, SPEC_B // 8, chunk, 0)
        for q in range(8):
            value = filt[pl.ds(q, SPEC, stride=8), :]
            high = value.astype(jnp.bfloat16)
            low = (value - high.astype(jnp.float32)).astype(jnp.bfloat16)
            here = slice(q * 128, q * 128 + 128)
            other = slice((q ^ 1) * 128, (q ^ 1) * 128 + 128)
            for held, part in ((ghi, high), (glo, low)):
                held[:SPEC, here] = part
                held[SPEC:, other] = part if q % 2 else -part
        if pol == 0:
            loads[5].wait()
            loads[6].wait()
        total = rows_by(thi[...], ghi[...]) + (rows_by(tlo[...], ghi[...]) + rows_by(thi[...], glo[...]))
        return total.astype(jnp.bfloat16)

    def chosen(pol):
        picked = times(wsel[...].reshape(512, NCHAN), spectra(pol))
        return picked.astype(jnp.bfloat16).reshape(16, 32, WIDTH)

    def regroup(ref):
        return times(perm[...], ref[...].reshape(512, WIDTH)).astype(jnp.bfloat16).reshape(16, 32, WIDTH)

    loads[3].wait()
    choose(False)
    send_a[...] = chosen(0)
    pl.semaphore_wait(barrier, 31)
    each(lambda d: copy_za(d).start())
    recv_a[z] = send_a[z]

    choose(True)
    send_b[...] = chosen(1)
    each(lambda d: copy_xb(d).start())
    recv_b[o] = send_b[o]

    to = lax.broadcasted_iota(jnp.int32, (512, 512), 0)
    perm[...] = one_hot(
        (to % 16) * 32 + (to // 16 % 2) * 16 + to // 32 == lax.broadcasted_iota(jnp.int32, (512, 512), 1))
    loads[4].wait()
    placed = jnp.broadcast_to(asg_v[...], (128, 512)).T
    for t in range(4):
        k = lax.broadcasted_iota(jnp.int32, (512, 128), 1) + t * 128
        r, up, low = k // 256, k // 16 % 16, k % 16
        hot_a[:, t * 128 : t * 128 + 128] = one_hot(placed == low * 32 + up // 8 * 16 + r * 8 + up % 8)
        hot_b[:, t * 128 : t * 128 + 128] = one_hot(placed == up * 32 + low // 8 * 16 + r * 8 + low % 8)

    def ordered(hot, held, pol):
        for slot in range(2):
            lines = held[:, slot * 16 : slot * 16 + 16, :].reshape(512, WIDTH)
            value = times(hot[...], lines)
            for t in range(3):
                spread[slot, t, pl.ds(pol, 512, stride=2), :] = value[:, t * 128 : t * 128 + 128]

    each(lambda d: copy_xb(d).wait_recv())
    stage_b[...] = regroup(recv_b)
    each(lambda d: copy_zb(d).start())
    x_b[row * 16 + z] = stage_b[z]
    forward_b(z).start()

    each(lambda d: copy_za(d).wait_recv())
    stage_a[...] = regroup(recv_a)
    each(lambda d: copy_xa(d).start())
    x_a[row * 16 + o] = stage_a[o]

    each(lambda d: copy_xa(d).wait_recv())
    forward_a().start()

    def pass_on(i, carry):
        d = far(i)
        copy_zb(d).wait_recv()
        forward_b(later(z, 16 - d)).start()
        return carry

    forward_a().wait_recv()
    ordered(hot_a, x_a, 0)
    lax.fori_loop(0, 15, pass_on, 0)

    def arrived(block, carry):
        forward_b(block).wait_recv()
        return carry

    lax.fori_loop(0, 16, arrived, 0)
    ordered(hot_b, x_b, 1)
    for slot in range(2):
        for t in range(3):
            out[slot, :, t * 128 : t * 128 + 128] = spread[slot, t].astype(jnp.bfloat16)

    each(lambda d: copy_za(d).wait_send())
    each(lambda d: copy_xb(d).wait_send())
    each(lambda d: copy_zb(d).wait_send())
    each(lambda d: copy_xa(d).wait_send())
    forward_a().wait_send()

    def left(block, carry):
        forward_b(block).wait_send()
        return carry

    lax.fori_loop(0, 16, left, 0)


def exchange(volts, taps, owner_map, assign):
    high, low = dft_tables()
    held = lambda *shape: pltpu.VMEM(shape, jnp.bfloat16)
    dma = pltpu.SemaphoreType.DMA
    block = (16, 32, WIDTH)
    return pl.pallas_call(
        exchange_kernel,
        out_shape=jax.ShapeDtypeStruct((2, 1024, WIDTH), jnp.bfloat16),
        in_specs=[pl.BlockSpec(memory_space=pl.ANY)] * 6,
        out_specs=pl.BlockSpec(memory_space=pltpu.VMEM),
        scratch_shapes=[
            held(2, BATCHES, BLOCKS, 8, 128),
            pltpu.VMEM((TAPS, NFFT), jnp.float32),
            pltpu.VMEM((TAPS, 8, 128), jnp.float32),
            pltpu.VMEM((NCHAN,), jnp.int32),
            pltpu.VMEM((1, 512), jnp.int32),
            held(NCHAN, 2 * NFFT),
            held(NCHAN, 2 * NFFT),
            pltpu.VMEM((SPEC * 8, 128), jnp.float32),
            held(WIDTH, 2 * NFFT),
            held(WIDTH, 2 * NFFT),
            held(16, 32, NCHAN),
            held(512, 512),
            held(512, 512),
            held(512, 512),
            held(*block),
            held(*block),
            held(*block),
            held(*block),
            held(*block),
            held(*block),
            held(32, 32, WIDTH),
            held(32, 32, WIDTH),
            pltpu.VMEM((2, 3, 1024, 128), jnp.float32),
            dma((7,)),
            dma((16,)), dma((16,)), dma((16,)), dma((16,)), dma((16,)), dma((16,)), dma((16,)), dma((16,)),
            dma, dma, dma((16,)), dma((16,)),
        ],
        compiler_params=pltpu.CompilerParams(
            collective_id=0, has_side_effects=True, vmem_limit_bytes=61 << 20
        ),
        name="exchange",
    )(volts, taps, owner_map, assign, jnp.asarray(high), jnp.asarray(low))


def visibility_kernel(lines, out, mine, turned):
    half = lax.axis_index("row") * 512

    @pl.when(pl.program_id(1) == 0)
    def _():
        ours = lines[0, pl.ds(pl.multiple_of(half, 512), 512), :].astype(jnp.float32)
        first = lax.broadcasted_iota(jnp.int32, (512, WIDTH), 1) < SPEC
        rolled = pltpu.roll(ours, SPEC, 1)
        mine[...] = ours.astype(jnp.bfloat16)
        turned[...] = jnp.where(first, rolled, -rolled).astype(jnp.bfloat16)

    scale = 1.0 / math.sqrt(WIDTH)
    width = out.shape[3]
    across = lines[0, pl.ds(pl.multiple_of(pl.program_id(1) * width, width), width), :]
    out[0, 0] = (rows_by(mine[...], across) * scale).astype(jnp.bfloat16)
    out[0, 1] = (rows_by(turned[...], across) * scale).astype(jnp.bfloat16)


def visibilities(lines):
    width = 256
    return pl.pallas_call(
        visibility_kernel,
        grid=(2, 1024 // width),
        out_shape=jax.ShapeDtypeStruct((2, 2, 512, 1024), jnp.bfloat16),
        in_specs=[pl.BlockSpec((1, 1024, WIDTH), lambda slot, j: (slot, 0, 0))],
        out_specs=pl.BlockSpec((1, 2, 512, width), lambda slot, j: (slot, 0, 0, j)),
        scratch_shapes=[pltpu.VMEM((512, WIDTH), jnp.bfloat16)] * 2,
        compiler_params=pltpu.CompilerParams(vmem_limit_bytes=61 << 20),
        name="visibilities",
    )(lines)


def shards(volts, taps, owner_map, assign):
    blocks = volts.reshape(BATCHES, 2, 2, BLOCKS, 4, 128).transpose(0, 1, 3, 4, 2, 5)
    lines = exchange(
        blocks.reshape(BATCHES, 2, BLOCKS, 8, 128),
        taps,
        owner_map,
        assign.reshape(1, 512),
    )
    return visibilities(lines)


def solution(mesh):
    placed = (P(None, ("chan", "row", "col"), None, None), P(), P(), P())
    return jax.shard_map(
        shards,
        mesh=mesh,
        in_specs=placed,
        out_specs=P(("chan", "col"), None, "row", None),
        check_vma=False,
    )
```

time: 181 us -> 65.4 us (0.36)
  Pallas kernels: 0 us -> 65.1 us
  waiting for transfers between devices: 56.1 us -> 0 us
  local copies, waits for them, and re-layouts: 44.2 us -> 0 us
  starting transfers between devices: 34.6 us -> 0 us
  matrix products: 19.4 us -> 0 us
  other arithmetic: 15.6 us -> 0 us
  blocking collectives: 10.1 us -> 0 us
    pallas_call x0 -> x2, Pallas kernels: none -> 65.1 us  [the longest x1 57.4 us: exchange(): pl.pallas_call(exchange_kernel, out_shape=jax.ShapeDtypeStruct((2, 1024,...]
    all_to_all x4 -> x0, waiting for transfers between devices: 56.1 us -> none  [the longest x2 47.3 us: shards(): lax.all_to_all(result.reshape(CAP, chan_count, cols_count, local_inputs,...]
    all_to_all x4 -> x0, starting transfers between devices: 34.6 us -> none  [the longest x2 22.3 us: shards(): lax.all_to_all(result.reshape(CAP, chan_count, cols_count, local_inputs,...]
    gather x9 -> x0, local copies, waits for them, and re-layouts: 27.5 us -> none  [the longest x4 8.64 us: shards(): rows = jnp.take(flat, row_pick, axis=1)]
    dot_general x4 -> x0, matrix products: 19.4 us -> none  [the longest x2 13.8 us: shards(): jnp.einsum('iasj,ajbkg->kgibs', summed, table, precision=lax.Precision.HI...]
    all_gather x2 -> x0, blocking collectives: 10.1 us -> none  [shards(): gathered = lax.all_gather(turned, 'row', axis=3, tiled=True)]
    convert_element_type x8 -> x0, local copies, waits for them, and re-layouts: 9.89 us -> none  [the longest x6 6.82 us: shards(): result.reshape(CAP, chan_count, cols_count, local_inputs, 2 * spec_len)]
    select_n x5 -> x0, other arithmetic: 4.55 us -> none  [the longest x1 4.24 us: shards(): columns = jnp.take(flat, located, axis=1)]
  transfers between devices with their start and end apart: 4 -> 0, of which waited for: 4 -> 0; matrix products, arithmetic and copies ran while one was open for 12% -> 0% of each run, Pallas kernels for 0% -> 0%
where the time goes in v1:
time: 65.4 us; the launch traced here: 65.2 us
  Pallas kernels  65.1 us (100%)
    pallas_call x1, Pallas kernels, exchange(): pl.pallas_call(exchange_kernel, out_shape=jax.ShapeDtypeStruct((2, 1024,...  57.4 us
    pallas_call x1, Pallas kernels, visibilities(): pl.pallas_call(visibility_kernel, grid=(2, 1024 // width), out_shape=jax....  7.71 us

profile of v1, /device:TPU:1, one launch (start us, length us, event | category | flops | bytes accessed | tf_op | source)
XLA Modules:
  0.0 65.2 jit_solution(15198558610314006119)
XLA Ops:
  0.0 57.4 %exchange.1.lines = bf16[2,1024,384]{2,1,0:T(8,128)(2,1)} custom-call(bf16[2,2,103,8,128]{4,3,2,1,0:T(8,128)(2,1)} %bitcast.6, f32[8,512]{1,0:T(8,128)} %taps.1, s32[384]{0:T(512)} %owner.1, s32[1,512]{1,0:T(1,128)} %bitcast.7, bf16[384,1024]{1,0:T(8,128)(2,1)} %constant.4.clone.table_hi, bf16[384,1024]{1,0:T(8,128)(2,1)} %constant.5.clone.table_lo), custom_call_target="tpu_custom_call" | custom-call | tf_op jit(solution)/shard_map/exchange/pallas_call | solution.py:262
  57.4 7.7 %visibilities.1 = bf16[2,2,512,1024]{3,2,1,0:T(8,128)(2,1)} custom-call(bf16[2,1024,384]{2,1,0:T(8,128)(2,1)} %exchange.1.lines), custom_call_target="tpu_custom_call" | custom-call | tf_op jit(solution)/shard_map/visibilities/pallas_call | solution.py:322

commit v2 on v1

--- a/solution.py
+++ b/solution.py
@@ -47,8 +47,8 @@
 def exchange_kernel(
     volts, taps, owner, assign, table_hi, table_lo, out,
     vbuf, tap_v, tapx, own_v, asg_v, thi, tlo, filt, ghi, glo, wsel, perm, hot_a, hot_b,
-    send_a, send_b, recv_a, recv_b, stage_a, stage_b, x_a, x_b, spread,
-    lsem, za_s, za_r, xb_s, xb_r, zb_s, zb_r, xa_s, xa_r, fa_s, fa_r, fb_s, fb_r,
+    send_a, send_b, recv_a, recv_b, stage_a, stage_b, x_a, x_b, spread, made,
+    ready, lsem, osem, za_s, za_r, xb_s, xb_r, zb_s, zb_r, xa_s, xa_r, fa_s, fa_r, fb_s, fb_r,
 ):
     chan, row, col = lax.axis_index("chan"), lax.axis_index("row"), lax.axis_index("col")
     z, o = chan // 2, chan % 2 * 8 + col
@@ -63,10 +63,15 @@
 
     def greet(d, carry):
         pl.semaphore_signal(barrier, inc=1, device_id=device(later(z, d), o, row), device_id_type=MESH)
+        pl.semaphore_signal(barrier, inc=1, device_id=device(later(z, 16 - d), o, row), device_id_type=MESH)
+        return carry
+
+    def greet_plane(d, carry):
         pl.semaphore_signal(barrier, inc=1, device_id=device(z, later(o, d), row), device_id_type=MESH)
         return carry
 
-    lax.fori_loop(1, 16, greet, 0)
+    lax.fori_loop(1, 5, greet, 0)
+    lax.fori_loop(1, 16, greet_plane, 0)
     pl.semaphore_signal(barrier, inc=1, device_id=device(z, o, 1 - row), device_id_type=MESH)
 
     loads = [
@@ -180,13 +185,27 @@
     loads[3].wait()
     choose(False)
     send_a[...] = chosen(0)
-    pl.semaphore_wait(barrier, 31)
-    each(lambda d: copy_za(d).start())
+    pl.semaphore_wait(barrier, 24)
+    for d in (4, 12):
+        pl.semaphore_signal(ready, inc=1, device_id=device(later(z, d), o, row), device_id_type=MESH)
+
+    def start_near(d, carry):
+        copy_za(d).start()
+        copy_za(16 - d).start()
+        return carry
+
+    def start_far(d, carry):
+        copy_za(d).start()
+        return carry
+
+    lax.fori_loop(1, 5, start_near, 0)
     recv_a[z] = send_a[z]
 
     choose(True)
     send_b[...] = chosen(1)
     each(lambda d: copy_xb(d).start())
+    pl.semaphore_wait(ready, 2)
+    lax.fori_loop(5, 12, start_far, 0)
     recv_b[o] = send_b[o]
 
     to = lax.broadcasted_iota(jnp.int32, (512, 512), 0)
@@ -237,9 +256,11 @@
 
     lax.fori_loop(0, 16, arrived, 0)
     ordered(hot_b, x_b, 1)
+    stores = [pltpu.make_async_copy(made.at[slot], out.at[slot], osem.at[slot]) for slot in range(2)]
     for slot in range(2):
         for t in range(3):
-            out[slot, :, t * 128 : t * 128 + 128] = spread[slot, t].astype(jnp.bfloat16)
+            made[slot, :, t * 128 : t * 128 + 128] = spread[slot, t].astype(jnp.bfloat16)
+        stores[slot].start()
 
     each(lambda d: copy_za(d).wait_send())
     each(lambda d: copy_xb(d).wait_send())
@@ -252,6 +273,8 @@
         return carry
 
     lax.fori_loop(0, 16, left, 0)
+    for store in stores:
+        store.wait()
 
 
 def exchange(volts, taps, owner_map, assign):
@@ -263,7 +286,7 @@
         exchange_kernel,
         out_shape=jax.ShapeDtypeStruct((2, 1024, WIDTH), jnp.bfloat16),
         in_specs=[pl.BlockSpec(memory_space=pl.ANY)] * 6,
-        out_specs=pl.BlockSpec(memory_space=pltpu.VMEM),
+        out_specs=pl.BlockSpec(memory_space=pl.ANY),
         scratch_shapes=[
             held(2, BATCHES, BLOCKS, 8, 128),
             pltpu.VMEM((TAPS, NFFT), jnp.float32),
@@ -288,45 +311,54 @@
             held(32, 32, WIDTH),
             held(32, 32, WIDTH),
             pltpu.VMEM((2, 3, 1024, 128), jnp.float32),
-            dma((7,)),
+            held(2, 1024, WIDTH),
+            pltpu.SemaphoreType.REGULAR,
+            dma((7,)), dma((2,)),
             dma((16,)), dma((16,)), dma((16,)), dma((16,)), dma((16,)), dma((16,)), dma((16,)), dma((16,)),
             dma, dma, dma((16,)), dma((16,)),
         ],
         compiler_params=pltpu.CompilerParams(
-            collective_id=0, has_side_effects=True, vmem_limit_bytes=61 << 20
+            collective_id=0, has_side_effects=True, vmem_limit_bytes=60 << 20
         ),
         name="exchange",
     )(volts, taps, owner_map, assign, jnp.asarray(high), jnp.asarray(low))
 
 
-def visibility_kernel(lines, out, mine, turned):
-    half = lax.axis_index("row") * 512
-
-    @pl.when(pl.program_id(1) == 0)
-    def _():
-        ours = lines[0, pl.ds(pl.multiple_of(half, 512), 512), :].astype(jnp.float32)
-        first = lax.broadcasted_iota(jnp.int32, (512, WIDTH), 1) < SPEC
-        rolled = pltpu.roll(ours, SPEC, 1)
-        mine[...] = ours.astype(jnp.bfloat16)
+def visibility_kernel(lines, out, held, turned, made, lsem, osem):
+    loads = [pltpu.make_async_copy(lines.at[slot], held.at[slot], lsem.at[slot]) for slot in range(2)]
+    for load in loads:
+        load.start()
+    half = pl.multiple_of(lax.axis_index("row") * 512, 512)
+    first = lax.broadcasted_iota(jnp.int32, (512, WIDTH), 1) < SPEC
+    scale = 1.0 / math.sqrt(WIDTH)
+    stores = []
+    for slot in range(2):
+        loads[slot].wait()
+        rolled = pltpu.roll(held[slot, pl.ds(half, 512), :].astype(jnp.float32), SPEC, 1)
         turned[...] = jnp.where(first, rolled, -rolled).astype(jnp.bfloat16)
-
-    scale = 1.0 / math.sqrt(WIDTH)
-    width = out.shape[3]
-    across = lines[0, pl.ds(pl.multiple_of(pl.program_id(1) * width, width), width), :]
-    out[0, 0] = (rows_by(mine[...], across) * scale).astype(jnp.bfloat16)
-    out[0, 1] = (rows_by(turned[...], across) * scale).astype(jnp.bfloat16)
+        for part in range(2):
+            ours = turned[...] if part else held[slot, pl.ds(half, 512), :]
+            made[slot, part] = (rows_by(ours, held[slot]) * scale).astype(jnp.bfloat16)
+            stores.append(pltpu.make_async_copy(made.at[slot, part], out.at[slot, part], osem.at[2 * slot + part]))
+            stores[-1].start()
+    for store in stores:
+        store.wait()
 
 
 def visibilities(lines):
-    width = 256
     return pl.pallas_call(
         visibility_kernel,
-        grid=(2, 1024 // width),
         out_shape=jax.ShapeDtypeStruct((2, 2, 512, 1024), jnp.bfloat16),
-        in_specs=[pl.BlockSpec((1, 1024, WIDTH), lambda slot, j: (slot, 0, 0))],
-        out_specs=pl.BlockSpec((1, 2, 512, width), lambda slot, j: (slot, 0, 0, j)),
-        scratch_shapes=[pltpu.VMEM((512, WIDTH), jnp.bfloat16)] * 2,
-        compiler_params=pltpu.CompilerParams(vmem_limit_bytes=61 << 20),
+        in_specs=[pl.BlockSpec(memory_space=pl.ANY)],
+        out_specs=pl.BlockSpec(memory_space=pl.ANY),
+        scratch_shapes=[
+            pltpu.VMEM((2, 1024, WIDTH), jnp.bfloat16),
+            pltpu.VMEM((512, WIDTH), jnp.bfloat16),
+            pltpu.VMEM((2, 2, 512, 1024), jnp.bfloat16),
+            pltpu.SemaphoreType.DMA((2,)),
+            pltpu.SemaphoreType.DMA((4,)),
+        ],
+        compiler_params=pltpu.CompilerParams(vmem_limit_bytes=60 << 20),
         name="visibilities",
     )(lines)
 

time: 65.4 us -> 61.1 us (0.934)
  Pallas kernels: 65.1 us -> 60.9 us
    pallas_call x1, Pallas kernels: 7.71 us -> 4.73 us  [visibilities(): pl.pallas_call(visibility_kernel, out_shape=jax.ShapeDtypeStruct((2, 2, 5...]
    pallas_call x1, Pallas kernels: 57.4 us -> 56.2 us  [exchange(): pl.pallas_call(exchange_kernel, out_shape=jax.ShapeDtypeStruct((2, 1024,...]
where the time goes in v2:
time: 61.1 us; the launch traced here: 60.9 us
  Pallas kernels  60.9 us (100%)
    pallas_call x1, Pallas kernels, exchange(): pl.pallas_call(exchange_kernel, out_shape=jax.ShapeDtypeStruct((2, 1024,...  56.2 us
    pallas_call x1, Pallas kernels, visibilities(): pl.pallas_call(visibility_kernel, out_shape=jax.ShapeDtypeStruct((2, 2, 5...  4.73 us

profile of v2, /device:TPU:1, one launch (start us, length us, event | category | flops | bytes accessed | tf_op | source)
XLA Modules:
  0.0 60.9 jit_solution(8021492364215777433)
XLA Ops:
  0.0 56.2 %exchange.1.lines = bf16[2,1024,384]{2,1,0:T(8,128)(2,1)} custom-call(bf16[2,2,103,8,128]{4,3,2,1,0:T(8,128)(2,1)} %bitcast.6, f32[8,512]{1,0:T(8,128)} %taps.1, s32[384]{0:T(512)} %owner.1, s32[1,512]{1,0:T(1,128)} %bitcast.7, bf16[384,1024]{1,0:T(8,128)(2,1)} %constant.4.clone.table_hi, bf16[384,1024]{1,0:T(8,128)(2,1)} %constant.5.clone.table_lo), custom_call_target="tpu_custom_call" | custom-call | tf_op jit(solution)/shard_map/exchange/pallas_call | solution.py:285
  56.2 4.7 %visibilities.1 = bf16[2,2,512,1024]{3,2,1,0:T(8,128)(2,1)} custom-call(bf16[2,1024,384]{2,1,0:T(8,128)(2,1)} %exchange.1.lines), custom_call_target="tpu_custom_call" | custom-call | tf_op jit(solution)/shard_map/visibilities/pallas_call | solution.py:349

commit v3 on v2

v3 whole, which is shorter than its diff:
```python
import functools
import math

import jax
import jax.numpy as jnp
import ml_dtypes
import numpy as np
from jax import lax
from jax.experimental import pallas as pl
from jax.experimental.pallas import tpu as pltpu
from jax.sharding import PartitionSpec as P

NFFT = 512
TAPS = 8
BATCHES = 2
SPEC_B = 96
NCHAN = 384
BLOCKS = SPEC_B + TAPS - 1
SPEC = BATCHES * SPEC_B
WIDTH = 2 * SPEC
MESH = pl.DeviceIdType.MESH


CLASSES = 4
PER_CLASS = NCHAN // CLASSES


def dft_tables():
    channel = np.arange(PER_CLASS)[None, :, None] * CLASSES + np.arange(CLASSES)[:, None, None]
    phase = 2.0 * np.pi / NFFT * (channel * np.arange(128) % NFFT)
    both = np.concatenate([np.cos(phase), np.sin(phase)], axis=2) / math.sqrt(NFFT)
    high = both.astype(np.float32).astype(ml_dtypes.bfloat16)
    low = (both - high.astype(np.float64)).astype(np.float32).astype(ml_dtypes.bfloat16)
    return np.concatenate([high, low], axis=1)


def rows_by(left, right):
    return lax.dot_general(
        left, right, (((1,), (1,)), ((), ())), preferred_element_type=jnp.float32
    )


def times(left, right):
    return jnp.dot(left, right, preferred_element_type=jnp.float32)


def one_hot(found):
    return jnp.where(found, 1.0, 0.0).astype(jnp.bfloat16)


def exchange_kernel(
    volts, taps, owner, assign, table, out,
    vbuf, tap_v, tapx, own_v, asg_v, tab_v, owners, before, filt, ghi, glo, spec, wsel, perm, hot_a, hot_b,
    send_a, send_b, recv_a, recv_b, stage_a, stage_b, x_a, x_b, partial, spread, made,
    ready, lsem, osem, za_s, za_r, xb_s, xb_r, zb_s, zb_r, xa_s, xa_r, fa_s, fa_r, fb_s, fb_r,
):
    chan, row, col = lax.axis_index("chan"), lax.axis_index("row"), lax.axis_index("col")
    z, o = chan // 2, chan % 2 * 8 + col

    def device(zz, oo, rr):
        return (zz * 2 + oo // 8, rr, oo % 8)

    def later(base, step):
        return lax.rem(base + step, 16)

    loads = [
        pltpu.make_async_copy(volts.at[:, 0], vbuf.at[0], lsem.at[0]),
        pltpu.make_async_copy(volts.at[:, 1], vbuf.at[1], lsem.at[1]),
        pltpu.make_async_copy(taps, tap_v, lsem.at[2]),
        pltpu.make_async_copy(owner, own_v, lsem.at[3]),
        pltpu.make_async_copy(assign, asg_v, lsem.at[4]),
        pltpu.make_async_copy(table, tab_v, lsem.at[5]),
    ]
    for k in (3, 0, 2, 5, 1, 4):
        loads[k].start()

    barrier = pltpu.get_barrier_semaphore()

    def greet(d, carry):
        pl.semaphore_signal(barrier, inc=1, device_id=device(later(z, d), o, row), device_id_type=MESH)
        pl.semaphore_signal(barrier, inc=1, device_id=device(later(z, 16 - d), o, row), device_id_type=MESH)
        return carry

    def greet_plane(d, carry):
        pl.semaphore_signal(barrier, inc=1, device_id=device(z, later(o, d), row), device_id_type=MESH)
        return carry

    lax.fori_loop(1, 5, greet, 0)
    lax.fori_loop(1, 16, greet_plane, 0)
    pl.semaphore_signal(barrier, inc=1, device_id=device(z, o, 1 - row), device_id_type=MESH)

    def far(i):
        return 8 + (1 - 2 * lax.rem(i, 2)) * ((i + 1) // 2)

    def copy_za(d):
        t = later(z, d)
        return pltpu.make_async_remote_copy(
            send_a.at[t], recv_a.at[z], za_s.at[d], za_r.at[d], device_id=device(t, o, row), device_id_type=MESH)

    def copy_xb(d):
        t = later(o, d)
        return pltpu.make_async_remote_copy(
            send_b.at[t], recv_b.at[o], xb_s.at[d], xb_r.at[d], device_id=device(z, t, row), device_id_type=MESH)

    def copy_zb(d):
        t = later(z, d)
        return pltpu.make_async_remote_copy(
            stage_b.at[t], x_b.at[z], zb_s.at[d], zb_r.at[d], device_id=device(t, o, row), device_id_type=MESH)

    def copy_xa(d):
        t = later(o, d)
        return pltpu.make_async_remote_copy(
            stage_a.at[t], x_a.at[o], xa_s.at[d], xa_r.at[d], device_id=device(z, t, row), device_id_type=MESH)

    def forward_a():
        return pltpu.make_async_remote_copy(
            x_a.at[pl.ds(0, 16)], x_a.at[pl.ds(16, 16)], fa_s, fa_r, device_id=device(z, o, 1 - row), device_id_type=MESH)

    def forward_b(block):
        return pltpu.make_async_remote_copy(
            x_b.at[block], x_b.at[16 + block], fb_s, fb_r,
            device_id=device(z, o, 1 - row), device_id_type=MESH)

    def each(action):
        def step(i, carry):
            action(far(i))
            return carry

        lax.fori_loop(0, 15, step, 0)

    def choose(swapped):
        line = lax.broadcasted_iota(jnp.int32, (256, NCHAN), 0)
        owner_of_line = (line % 16) * 16 + line // 16 if swapped else line
        owned = jnp.where(owners[0:1, :] == owner_of_line.astype(jnp.float32), 1.0, 0.0)
        earlier = times(owned.astype(jnp.bfloat16), before[...])
        for slot in range(2):
            taken = jnp.where(earlier == float(slot), owned, 0.0).astype(jnp.bfloat16)
            wsel[:, slot * 16 : slot * 16 + 16, :] = taken.reshape(16, 16, NCHAN)

    def spectra(pol):
        loads[pol].wait()
        if pol == 0:
            loads[2].wait()
            for m in range(TAPS):
                for j in range(4):
                    line = tap_v[m : m + 1, j * 128 : j * 128 + 128]
                    tapx[m, 2 * j : 2 * j + 2, :] = jnp.broadcast_to(line, (2, 128))
        weights = [tapx[m] for m in range(TAPS)]

        def chunk(i, carry):
            first = i * 8
            for b in range(BATCHES):
                signal = [vbuf[pol, b, first + t].astype(jnp.float32) for t in range(15)]
                for s in range(8):
                    total = weights[0] * signal[s]
                    for m in range(1, TAPS):
                        total = total + weights[m] * signal[s + m]
                    filt[pl.ds(pl.multiple_of((b * SPEC_B + first + s) * 8, 8), 8), :] = total
            return carry

        lax.fori_loop(0, SPEC_B // 8, chunk, 0)
        for top in range(0, SPEC, 32):
            x = [filt[pl.ds(8 * top + q, 32, stride=8), :] for q in range(8)]
            (er, ei), (dr, di) = ((x[0] + x[4], x[1] + x[5]), (x[0] - x[4], x[1] - x[5]))
            (fr, fi), (gr, gi) = ((x[2] + x[6], x[3] + x[7]), (x[2] - x[6], x[3] - x[7]))
            folded = ((er + fr, ei + fi), (dr + gi, di - gr), (er - fr, ei - fi), (dr - gi, di + gr))
            for r in range(CLASSES):
                for a in range(2):
                    value = folded[r][a]
                    high = value.astype(jnp.bfloat16)
                    low = (value - high.astype(jnp.float32)).astype(jnp.bfloat16)
                    here, other = slice(a * 128, a * 128 + 128), slice(128 - a * 128, 256 - a * 128)
                    for held, part in ((ghi, high), (glo, low)):
                        held[r, top : top + 32, here] = part
                        held[r, SPEC + top : SPEC + top + 32, other] = part if a else -part
        if pol == 0:
            loads[5].wait()
        for r in range(CLASSES):
            both = rows_by(tab_v[r], ghi[r])
            small = rows_by(tab_v[r, :PER_CLASS], glo[r])
            total = both[:PER_CLASS] + (both[PER_CLASS:] + small)
            spec[r * PER_CLASS : r * PER_CLASS + PER_CLASS, :] = total.astype(jnp.bfloat16)

    def chosen(pol):
        spectra(pol)
        picked = times(wsel[...].reshape(512, NCHAN), spec[...])
        return picked.astype(jnp.bfloat16).reshape(16, 32, WIDTH)

    def regroup(ref):
        return times(perm[...], ref[...].reshape(512, WIDTH)).astype(jnp.bfloat16).reshape(16, 32, WIDTH)

    loads[3].wait()
    def channel_at(axis):
        i = lax.broadcasted_iota(jnp.int32, (NCHAN, NCHAN), axis)
        steps = [jnp.where(i >= r * PER_CLASS, 1, 0) for r in range(1, CLASSES)]
        return 4 * i - (NCHAN - 1) * (steps[0] + steps[1] + steps[2])

    moved = one_hot(lax.broadcasted_iota(jnp.int32, (NCHAN, NCHAN), 0) == channel_at(1))
    line = jnp.broadcast_to(own_v[...].reshape(1, NCHAN), (8, NCHAN))
    owners[...] = times(line.astype(jnp.float32).astype(jnp.bfloat16), moved)
    before[...] = one_hot(channel_at(0) < channel_at(1))
    choose(False)
    send_a[...] = chosen(0)
    pl.semaphore_wait(barrier, 24)
    for d in (4, 12):
        pl.semaphore_signal(ready, inc=1, device_id=device(later(z, d), o, row), device_id_type=MESH)

    def start_near(d, carry):
        copy_za(d).start()
        copy_za(16 - d).start()
        return carry

    def start_far(i, carry):
        copy_za(far(i)).start()
        return carry

    lax.fori_loop(1, 5, start_near, 0)
    recv_a[z] = send_a[z]

    choose(True)
    send_b[...] = chosen(1)
    each(lambda d: copy_xb(d).start())
    pl.semaphore_wait(ready, 2)
    lax.fori_loop(0, 7, start_far, 0)
    recv_b[o] = send_b[o]

    to = lax.broadcasted_iota(jnp.int32, (512, 512), 0)
    perm[...] = one_hot(
        (to % 16) * 32 + (to // 16 % 2) * 16 + to // 32 == lax.broadcasted_iota(jnp.int32, (512, 512), 1))
    loads[4].wait()
    placed = jnp.broadcast_to(asg_v[...], (128, 512)).T
    for t in range(4):
        k = lax.broadcasted_iota(jnp.int32, (512, 128), 1) + t * 128
        r, up, low = row if t < 2 else 1 - row, k // 16 % 16, k % 16
        hot_a[:, t * 128 : t * 128 + 128] = one_hot(placed == low * 32 + up // 8 * 16 + r * 8 + up % 8)
        hot_b[:, t * 128 : t * 128 + 128] = one_hot(placed == up * 32 + low // 8 * 16 + r * 8 + low % 8)

    def lines_of(held, slot, first, last):
        return held[first:last, slot * 16 : slot * 16 + 16, :].reshape((last - first) * 16, WIDTH)

    def ordered(pol, slot):
        if pol:
            value = partial[slot] + times(hot_b[:, 256:], lines_of(x_b, slot, 16, 32))
        else:
            value = times(hot_a[...], lines_of(x_a, slot, 0, 32))
        for t in range(3):
            spread[slot, t, pl.ds(pol, 512, stride=2), :] = value[:, t * 128 : t * 128 + 128]

    each(lambda d: copy_xb(d).wait_recv())
    stage_b[...] = regroup(recv_b)
    each(lambda d: copy_za(d).wait_send())
    def start_zb(group):
        def step(i, carry):
            t = group * 8 + lax.rem(z + 4 + i, 8)

            @pl.when(t != z)
            def _():
                copy_zb(later(t, 16 - z)).start()

            return carry

        lax.fori_loop(0, 8, step, 0)

    for group in (0,):
        start_zb(group)
    x_b[z] = stage_b[z]
    forward_b(z).start()

    each(lambda d: copy_za(d).wait_recv())
    stage_a[...] = regroup(recv_a)
    each(lambda d: copy_xa(d).start())
    for group in (1,):
        start_zb(group)
    x_a[o] = stage_a[o]

    each(lambda d: copy_xb(d).wait_send())
    each(lambda d: copy_xa(d).wait_recv())
    forward_a().start()
    each(lambda d: copy_xa(d).wait_send())

    def pass_on(i, carry):
        d = far(i)
        copy_zb(d).wait()
        forward_b(later(z, 16 - d)).start()
        return carry

    forward_a().wait()
    for slot in range(2):
        ordered(0, slot)
    lax.fori_loop(0, 15, pass_on, 0)
    for slot in range(2):
        partial[slot] = times(hot_b[:, :256], lines_of(x_b, slot, 0, 16))

    pltpu.make_async_copy(x_b.at[pl.ds(16, 16)], x_b.at[pl.ds(16, 16)], fb_r).wait()
    stores = [pltpu.make_async_copy(made.at[slot], out.at[slot], osem.at[slot]) for slot in range(2)]
    for slot in range(2):
        ordered(1, slot)
        for t in range(3):
            made[slot, :, t * 128 : t * 128 + 128] = spread[slot, t].astype(jnp.bfloat16)
        stores[slot].start()
    pltpu.make_async_copy(x_b.at[pl.ds(0, 16)], x_b.at[pl.ds(0, 16)], fb_s).wait()
    for store in stores:
        store.wait()


def exchange(volts, taps, owner_map, assign):
    held = lambda *shape: pltpu.VMEM(shape, jnp.bfloat16)
    dma = pltpu.SemaphoreType.DMA
    block = (16, 32, WIDTH)
    return pl.pallas_call(
        exchange_kernel,
        out_shape=jax.ShapeDtypeStruct((2, 1024, WIDTH), jnp.bfloat16),
        in_specs=[pl.BlockSpec(memory_space=pl.ANY)] * 5,
        out_specs=pl.BlockSpec(memory_space=pl.ANY),
        scratch_shapes=[
            held(2, BATCHES, BLOCKS, 8, 128),
            pltpu.VMEM((TAPS, NFFT), jnp.float32),
            pltpu.VMEM((TAPS, 8, 128), jnp.float32),
            pltpu.VMEM((NCHAN,), jnp.int32),
            pltpu.VMEM((1, 512), jnp.int32),
            held(CLASSES, 2 * PER_CLASS, 256),
            pltpu.VMEM((8, NCHAN), jnp.float32),
            held(NCHAN, NCHAN),
            pltpu.VMEM((SPEC * 8, 128), jnp.float32),
            held(CLASSES, WIDTH, 256),
            held(CLASSES, WIDTH, 256),
            held(NCHAN, WIDTH),
            held(16, 32, NCHAN),
            held(512, 512),
            held(512, 512),
            held(512, 512),
            held(*block),
            held(*block),
            held(*block),
            held(*block),
            held(*block),
            held(*block),
            held(32, 32, WIDTH),
            held(32, 32, WIDTH),
            pltpu.VMEM((2, 512, WIDTH), jnp.float32),
            pltpu.VMEM((2, 3, 1024, 128), jnp.float32),
            held(2, 1024, WIDTH),
            pltpu.SemaphoreType.REGULAR,
            dma((6,)), dma((2,)),
            dma((16,)), dma((16,)), dma((16,)), dma((16,)), dma((16,)), dma((16,)), dma((16,)), dma((16,)),
            dma, dma, dma, dma,
        ],
        compiler_params=pltpu.CompilerParams(
            collective_id=0, has_side_effects=True, vmem_limit_bytes=60 << 20
        ),
        name="exchange",
    )(volts, taps, owner_map, assign, jnp.asarray(dft_tables()))


def visibility_kernel(lines, out, held, turned, made, lsem, osem):
    half = lax.axis_index("row") * 512
    loads = [pltpu.make_async_copy(lines.at[slot], held.at[slot], lsem.at[slot]) for slot in range(2)]
    for load in loads:
        load.start()
    first = lax.broadcasted_iota(jnp.int32, (512, WIDTH), 1) < SPEC
    scale = 1.0 / math.sqrt(WIDTH)
    stores = []
    for slot in range(2):
        loads[slot].wait()
        ours = held[slot, pl.ds(pl.multiple_of(half, 512), 512), :].astype(jnp.float32)
        rolled = pltpu.roll(ours, SPEC, 1)
        turned[slot] = jnp.where(first, rolled, -rolled).astype(jnp.bfloat16)
        for part in range(2):
            for top in (0, 256):
                rows = pl.ds(top, 256)
                left = turned[slot, rows] if part else held[slot, pl.ds(pl.multiple_of(half + top, 256), 256), :]
                made[slot, part, rows] = (rows_by(left, held[slot]) * scale).astype(jnp.bfloat16)
                stores.append(
                    pltpu.make_async_copy(made.at[slot, part, rows], out.at[slot, part, rows], osem.at[len(stores)]))
                stores[-1].start()
    for store in stores:
        store.wait()


def visibilities(lines):
    return pl.pallas_call(
        visibility_kernel,
        out_shape=jax.ShapeDtypeStruct((2, 2, 512, 1024), jnp.bfloat16),
        in_specs=[pl.BlockSpec(memory_space=pl.ANY)],
        out_specs=pl.BlockSpec(memory_space=pl.ANY),
        scratch_shapes=[
            pltpu.VMEM((2, 1024, WIDTH), jnp.bfloat16),
            pltpu.VMEM((2, 512, WIDTH), jnp.bfloat16),
            pltpu.VMEM((2, 2, 512, 1024), jnp.bfloat16),
            pltpu.SemaphoreType.DMA((2,)),
            pltpu.SemaphoreType.DMA((8,)),
        ],
        compiler_params=pltpu.CompilerParams(vmem_limit_bytes=60 << 20),
        name="visibilities",
    )(lines)


def shards(volts, taps, owner_map, assign):
    blocks = volts.reshape(BATCHES, 2, 2, BLOCKS, 4, 128).transpose(0, 1, 3, 4, 2, 5)
    lines = exchange(
        blocks.reshape(BATCHES, 2, BLOCKS, 8, 128),
        taps,
        owner_map,
        assign.reshape(1, 512),
    )
    return visibilities(lines)


def solution(mesh):
    placed = (P(None, ("chan", "row", "col"), None, None), P(), P(), P())
    return jax.shard_map(
        shards,
        mesh=mesh,
        in_specs=placed,
        out_specs=P(("chan", "col"), None, "row", None),
        check_vma=False,
    )
```

time: 61.1 us -> 61.8 us (1.011)
  the two profiles are of different devices: /device:TPU:1 before, /device:TPU:33 now
where the time goes in v3:
time: 61.8 us; the launch traced here: 61.6 us
  Pallas kernels  61.6 us (100%)
    pallas_call x1, Pallas kernels, exchange(): pl.pallas_call(exchange_kernel, out_shape=jax.ShapeDtypeStruct((2, 1024,...  57 us
    pallas_call x1, Pallas kernels, visibilities(): pl.pallas_call(visibility_kernel, out_shape=jax.ShapeDtypeStruct((2, 2, 5...  4.6 us

profile of v3, /device:TPU:33, one launch (start us, length us, event | category | flops | bytes accessed | tf_op | source)
XLA Modules:
  0.0 61.6 jit_solution(15924392497332456034)
XLA Ops:
  0.0 57.0 %exchange.1.lines = bf16[2,1024,384]{2,1,0:T(8,128)(2,1)} custom-call(bf16[2,2,103,8,128]{4,3,2,1,0:T(8,128)(2,1)} %bitcast.6, f32[8,512]{1,0:T(8,128)} %taps.1, s32[384]{0:T(512)} %owner.1, s32[1,512]{1,0:T(1,128)} %bitcast.7, bf16[4,192,256]{2,1,0:T(8,128)(2,1)} %constant.2.clone.table), custom_call_target="tpu_custom_call" | custom-call | tf_op jit(solution)/shard_map/exchange/pallas_call | solution.py:310
  57.0 4.6 %visibilities.1 = bf16[2,2,512,1024]{3,2,1,0:T(8,128)(2,1)} custom-call(bf16[2,1024,384]{2,1,0:T(8,128)(2,1)} %exchange.1.lines), custom_call_target="tpu_custom_call" | custom-call | tf_op jit(solution)/shard_map/visibilities/pallas_call | solution.py:381

commit v4 on v3

--- a/solution.py
+++ b/solution.py
@@ -249,28 +249,18 @@
     each(lambda d: copy_xb(d).wait_recv())
     stage_b[...] = regroup(recv_b)
     each(lambda d: copy_za(d).wait_send())
-    def start_zb(group):
-        def step(i, carry):
-            t = group * 8 + lax.rem(z + 4 + i, 8)
-
-            @pl.when(t != z)
-            def _():
-                copy_zb(later(t, 16 - z)).start()
-
-            return carry
-
-        lax.fori_loop(0, 8, step, 0)
-
-    for group in (0,):
-        start_zb(group)
+    def start_zb(i, carry):
+        copy_zb(far(i)).start()
+        return carry
+
+    lax.fori_loop(0, 7, start_zb, 0)
     x_b[z] = stage_b[z]
     forward_b(z).start()
 
     each(lambda d: copy_za(d).wait_recv())
     stage_a[...] = regroup(recv_a)
     each(lambda d: copy_xa(d).start())
-    for group in (1,):
-        start_zb(group)
+    lax.fori_loop(7, 15, start_zb, 0)
     x_a[o] = stage_a[o]
 
     each(lambda d: copy_xb(d).wait_send())

time: 61.8 us -> 60.4 us (0.977)
  the two profiles are of different devices: /device:TPU:33 before, /device:TPU:1 now
where the time goes in v4:
time: 60.4 us; the launch traced here: 60.2 us
  Pallas kernels  60.2 us (100%)
    pallas_call x1, Pallas kernels, exchange(): pl.pallas_call(exchange_kernel, out_shape=jax.ShapeDtypeStruct((2, 1024,...  55.6 us
    pallas_call x1, Pallas kernels, visibilities(): pl.pallas_call(visibility_kernel, out_shape=jax.ShapeDtypeStruct((2, 2, 5...  4.59 us

profile of v4, /device:TPU:1, one launch (start us, length us, event | category | flops | bytes accessed | tf_op | source)
XLA Modules:
  0.0 60.2 jit_solution(11489731614493161794)
XLA Ops:
  0.0 55.6 %exchange.1.lines = bf16[2,1024,384]{2,1,0:T(8,128)(2,1)} custom-call(bf16[2,2,103,8,128]{4,3,2,1,0:T(8,128)(2,1)} %bitcast.6, f32[8,512]{1,0:T(8,128)} %taps.1, s32[384]{0:T(512)} %owner.1, s32[1,512]{1,0:T(1,128)} %bitcast.7, bf16[4,192,256]{2,1,0:T(8,128)(2,1)} %constant.2.clone.table), custom_call_target="tpu_custom_call" | custom-call | tf_op jit(solution)/shard_map/exchange/pallas_call | solution.py:300
  55.6 4.6 %visibilities.1 = bf16[2,2,512,1024]{3,2,1,0:T(8,128)(2,1)} custom-call(bf16[2,1024,384]{2,1,0:T(8,128)(2,1)} %exchange.1.lines), custom_call_target="tpu_custom_call" | custom-call | tf_op jit(solution)/shard_map/visibilities/pallas_call | solution.py:371
